TPU v7x, 256 devices: a whole 4x4x8 slice. The times are simulated.
256 devices in a mesh: row: 32 (over x, y, core), col: 8 (over z).
Axes of the slice: x: 4, y: 4, z: 8, core: 2. Of those that a mesh axis runs over, the one named last changes fastest.
Arguments:
- solution: float32 [64, 65536], P(None, ('row', 'col')), may hold values from -6 to 6
- residual: float32 [64, 262144], P(None, ('row', 'col')), may hold values from -6 to 6
- direction: float32 [64, 65536], P(None, ('row', 'col')), may hold values from -6 to 6
- jacobian_tiles: bfloat16 [2048, 40, 128, 128], P('row', 'col'), may hold values from -0.078125 to 0.078125
- tile_blocks: int32 [2048, 40], P('row', 'col'), may hold values from 0 to 63, as said below
- tile_counts: int32 [2048, 8], P('row', 'col'), may hold values from 1 to 5, as said below
Outputs:
- solution_next: float32 [64, 65536], P(None, ('row', 'col'))
- residual_next: float32 [64, 262144], P(None, ('row', 'col'))
- direction_next: float32 [64, 65536], P(None, ('row', 'col'))
Inputs may be any that keep to these rules, and one draw needn't show every extreme that they name: `tile_blocks`: within each sensor and parameter group the 5 entries are different. Only the first tile_counts[i, c] slots of sensor i in group c hold a tile; some sensor fills all 5 slots of every group.
All inputs are finite; a program needn't handle non-finite values.
Results may differ from a plain program's by a relative error of at most 0.023.
Values may be sent and summed in bfloat16 or wider, within the bound.
A program may use at most 128 MiB of HBM per device.

v0:
```python
import functools
import jax
import jax.numpy as jnp
from jax import lax
from jax.sharding import Mesh
from jax.sharding import PartitionSpec as P

CB_DEV = 64
ITERS = 2
ROW = ("row_0", "row_1", "row_2")
ROW_COL = ("row_0", "row_1", "row_2", "col")


def in_blocks(value, dim, devices):
    before, after = (value.shape[:dim], value.shape[dim + 1 :])
    return jnp.moveaxis(value.reshape(*before, devices, -1, *after), dim, 0)


def sent_and_summed(value, axis, dim):
    devices = lax.axis_size(axis)
    tiles = lax.all_to_all(in_blocks(value, dim, devices), axis, 0, 0, tiled=True)
    return jnp.sum(tiles.astype(jnp.float32), axis=0)


def over_axes(value, axes):
    return functools.reduce(lax.psum, axes, value)


def laid_out(tiles, dim):
    tiles = jnp.moveaxis(tiles, 0, dim)
    lengths = tiles.shape
    return tiles.reshape(*lengths[:dim], lengths[dim] * lengths[dim + 1], *lengths[dim + 2 :])


def copy_for_each(value, axis):
    devices = lax.axis_size(axis)
    return lax.all_to_all(
        jnp.broadcast_to(value[None], (devices, *value.shape)), axis, 0, 0, tiled=True
    )


def collect(value, axis, dim):
    return laid_out(copy_for_each(value, axis), dim)


def times_highest(left, right):
    return jnp.dot(left, right, precision=lax.Precision.HIGHEST)


def gram_matrix(values):
    return jnp.dot(values, values.T, precision=lax.Precision.HIGHEST)


def solve_spd(matrix, right):
    factor_low = jnp.linalg.cholesky(matrix)
    middle = lax.linalg.triangular_solve(factor_low, right, left_side=True, lower=True)
    return lax.linalg.triangular_solve(
        factor_low, middle, left_side=True, lower=True, transpose_a=True
    )


def images(jacobian_tiles, tile_blocks, live_slot, direction_half):
    rhs_count = direction_half.shape[0]
    tile_width = jacobian_tiles.shape[2]
    table_view = direction_half.reshape(rhs_count, -1, tile_width)
    picked = jnp.take(table_view, tile_blocks, axis=1) * live_slot[None, :, :, None]
    product = jnp.einsum(
        "rsab,nrsb->nra", jacobian_tiles, picked, preferred_element_type=jnp.float32
    )
    return product.reshape(rhs_count, -1)


def gradients(jacobian_tiles, tile_blocks, live_slot, rows_half):
    rhs_count = rows_half.shape[0]
    tile_width = jacobian_tiles.shape[2]
    sensors = jacobian_tiles.shape[0]
    row_view = rows_half.reshape(rhs_count, sensors, tile_width)
    contrib = jnp.einsum(
        "rsab,nra->rsnb", jacobian_tiles, row_view, preferred_element_type=jnp.float32
    )
    contrib = contrib * live_slot.astype(jnp.float32)[:, :, None, None]
    summed = jax.ops.segment_sum(
        contrib.reshape(-1, rhs_count, tile_width), tile_blocks.reshape(-1), num_segments=CB_DEV
    )
    return summed.transpose(1, 0, 2).reshape(rhs_count, CB_DEV * tile_width)


def per_device(solution, residual, direction, jacobian_tiles, tile_blocks, tile_counts):
    live_slot = (
        jnp.arange(jacobian_tiles.shape[1], dtype=jnp.int32)[None, :] < tile_counts
    ).astype(jnp.bfloat16)
    share_rows = residual.shape[1]
    col_start = lax.axis_index("col") * share_rows
    rows_now = lax.all_gather(residual.astype(jnp.bfloat16), "col", axis=1, tiled=True).astype(
        residual.dtype
    )

    def gradient_step(rows_value):
        rows_half = rows_value.astype(jnp.bfloat16)
        partial_term = gradients(jacobian_tiles, tile_blocks, live_slot, rows_half)
        gradient = sent_and_summed(partial_term.astype(jnp.bfloat16), ROW, 1)
        gamma_value = over_axes(gram_matrix(gradient), ROW_COL)
        return (gradient, gamma_value)

    gradient, gamma_now = gradient_step(rows_now)
    iterate = solution
    for iteration in range(ITERS):
        direction_half = collect(direction.astype(jnp.bfloat16), ROW, 1)
        image_partial_term = images(jacobian_tiles, tile_blocks, live_slot, direction_half)
        image = lax.psum(image_partial_term.astype(jnp.bfloat16), "col").astype(jnp.float32)
        curvature = over_axes(gram_matrix(image), ROW)
        image, curvature = (image, curvature)
        step_alpha = solve_spd(curvature, gamma_now)
        iterate = iterate + times_highest(step_alpha.T, direction)
        rows_now = rows_now - times_highest(step_alpha.T, image)
        gradient, gamma_next = gradient_step(rows_now)
        step_beta = solve_spd(gamma_now, gamma_next)
        direction = gradient + times_highest(step_beta.T, direction)
        gamma_now = gamma_next
    residual_out = lax.dynamic_slice_in_dim(rows_now, col_start, share_rows, 1)
    return (iterate, residual_out, direction)


def solution(mesh):
    torus = Mesh(
        mesh.devices.reshape(4, 4, 2, mesh.shape["col"]), ("row_0", "row_1", "row_2", "col")
    )
    in_specs = (
        P(None, ROW_COL),
        P(None, ROW_COL),
        P(None, ROW_COL),
        P(ROW, "col", None, None),
        P(ROW, "col"),
        P(ROW, "col"),
    )
    out_specs = (P(None, ROW_COL), P(None, ROW_COL), P(None, ROW_COL))
    return jax.shard_map(
        per_device, mesh=torus, in_specs=in_specs, out_specs=out_specs, check_vma=False
    )
```

profile of v0, /device:TPU:4, one launch (start us, length us, event | category | flops | bytes accessed | tf_op | source)
XLA Modules:
  0.0 678.9 jit_solution(5240777342642542572)
XLA Ops:
  7.2 0.8 convert_element_type.98
  8.0 1.1 broadcast_in_dim.13
  9.1 7.6 %all-to-all-start = ((bf16[32,64,256]{2,1,0:T(8,128)(2,1)}), bf16[32,64,256]{2,1,0:T(8,128)(2,1)S(1)}, u32[]{:S(2)}, u32[]{:S(2)}) async-start(bf16[32,64,256]{2,1,0:T(8,128)(2,1)} %broadcast_in_dim.13), calls=%async_computation | async-start | bytes 2097152 | tf_op jit(solution)/shard_map/all_to_all | solution.py:37
  16.8 1.6 convert_element_type.103
  18.5 0.8 copy.74
  20.3 0.7 compare_and_fusion
  21.1 0.7 fusion.39
  21.9 9.7 %all-to-all-done = bf16[32,64,256]{2,1,0:T(8,128)(2,1)S(1)} async-done(((bf16[32,64,256]{2,1,0:T(8,128)(2,1)}), bf16[32,64,256]{2,1,0:T(8,128)(2,1)S(1)}, u32[]{:S(2)}, u32[]{:S(2)}) %all-to-all-start) | async-done | bytes 1048608 | tf_op jit(solution)/shard_map/all_to_all | solution.py:37
  33.3 13.3 %gather_fusion = bf16[320,64,128]{2,1,0:T(8,128)(2,1)} fusion(bf16[64,64,128]{2,0,1:T(8,128)(2,1)S(1)} %copy.70, s32[1024]{0:T(1024)S(1)} %pad_clamp_fusion), kind=kCustom, calls=%fused_computation.clone | custom fusion | bytes 10487040 | tf_op jit(solution)/shard_map/jit(_take)/gather | solution.py:66
  46.6 10.1 %fusion.10 = bf16[64,8,8,128]{3,2,1,0:T(8,128)(2,1)S(1)} fusion(bf16[64,5,128,128]{3,2,1,0:T(8,128)(2,1)} %param.16, bf16[64,5,64,128]{3,2,1,0:T(8,128)(2,1)} %bitcast.164, pred[64,5]{1,0:T(8,128)(4,1)S(1)} %copy.67, bf16[64,5]{1,0:T(8,128)(2,1)S(1)} %get-tuple-element.13), kind=kOutput, calls=%fused_computation.27 | convolution fusion | flops 676855808 | bytes 16778176 | tf_op jit(solution)/shard_map/rsab,nrsb->nra/dot_general | solution.py:67
  56.7 1.2 copy.124
  57.9 3.5 all-gather.2.cloned.1.call-done
  61.4 1.5 copy.112
  62.9 10.2 %broadcast_multiply_fusion.2 = f32[64,64,5,128]{3,1,2,0:T(8,128)} fusion(f32[64,5]{1,0:T(8,128)S(1)} %get-tuple-element.14, bf16[64,5,128,128]{3,2,1,0:T(8,128)(2,1)} %param.16, bf16[64,64,128,1]{2,1,0,3:T(8,128)(2,1)S(1)} %bitcast.166), kind=kOutput, calls=%fused_computation.15 | convolution fusion | flops 673710080 | bytes 22021376 | tf_op jit(solution)/shard_map/rsab,nra->rsnb/dot_general | solution.py:78
  73.3 33.3 %scatter_fusion = f32[64,64,128]{2,1,0:T(8,128)S(1)} fusion(f32[64,64,128]{2,1,0:T(8,128)S(1)} %broadcast.78.clone, s32[320]{0:T(512)S(1)} %reshape.148, f32[320,64,128]{2,1,0:T(8,128)} %bitcast.161), kind=kCustom, calls=%fused_computation.2 | custom fusion | flops 2621440 | bytes 31458560 | tf_op jit(solution)/shard_map/scatter-add | solution.py:82
  107.9 1.6 copy.77
  109.5 7.4 %all-to-all-start.1 = ((bf16[32,64,256]{2,1,0:T(8,128)(2,1)}), bf16[32,64,256]{2,1,0:T(8,128)(2,1)S(1)}, u32[]{:S(2)}, u32[]{:S(2)}) async-start(bf16[32,64,256]{2,1,0:T(8,128)(2,1)} %copy.77), calls=%async_computation.1 | async-start | bytes 2097152 | tf_op jit(solution)/shard_map/all_to_all | solution.py:21
  116.9 21.1 %all-reduce.6.cloned.1.call-done = bf16[64,8192]{1,0:T(8,128)(2,1)} async-done(((bf16[64,8192]{1,0:T(8,128)(2,1)}), bf16[64,8192]{1,0:T(8,128)(2,1)}) %all-reduce.6.cloned.1.call-update) | async-done | bytes 1048592 | tf_op jit(solution)/shard_map/psum | solution.py:110
  138.0 2.0 fusion.44
  140.3 16.0 %all-reduce.1 = (f32[64,64]{0,1:T(8,128)S(1)}, f32[64,64]{0,1:T(8,128)S(1)}) all-reduce(f32[64,64]{0,1:T(8,128)S(1)} %fusion.45, f32[64,64]{0,1:T(8,128)S(1)} %fusion.44), channel_id=1, replica_groups=mesh['row_0'=4,'row_1'=4,'row_2'=2,'col'=8] {'row_0'}, use_global_device_ids=true, to_apply=%region_8.0 | all-reduce | flops 8192 | bytes 65536 | tf_op jit(solution)/shard_map/psum | solution.py:26
  156.3 17.6 %all-reduce = (f32[64,64]{0,1:T(8,128)S(1)}, f32[64,64]{0,1:T(8,128)S(1)}) all-reduce(f32[64,64]{0,1:T(8,128)S(1)} %get-tuple-element.9, f32[64,64]{0,1:T(8,128)S(1)} %get-tuple-element.10), channel_id=1, replica_groups=mesh['row_0'=4,'row_1'=4,'row_2'=2,'col'=8] {'row_1'}, use_global_device_ids=true, to_apply=%region_9.0 | all-reduce | flops 8192 | bytes 65536 | tf_op jit(solution)/shard_map/psum | solution.py:26
  173.9 3.6 all-reduce.2
  177.5 29.1 %psum.147 = f32[64,64]{0,1:T(8,128)S(1)} all-reduce(f32[64,64]{0,1:T(8,128)S(1)} %get-tuple-element.11), channel_id=1, replica_groups=mesh['row_0'=4,'row_1'=4,'row_2'=2,'col'=8] {'col'}, use_global_device_ids=true, to_apply=%region_11.14 | all-reduce | flops 4096 | bytes 32768 | tf_op jit(solution)/shard_map/psum | solution.py:26
  206.7 5.8 cholesky.74
  213.9 4.9 custom-call.15
  219.2 2.3 convolution_subtract_fusion.1
  221.6 1.3 copy-done
  223.3 10.2 %broadcast_multiply_fusion.1 = f32[64,64,5,128]{3,1,2,0:T(8,128)} fusion(f32[64,5]{1,0:T(8,128)S(1)} %get-tuple-element.14, bf16[64,5,128,128]{3,2,1,0:T(8,128)(2,1)} %param.16, bf16[64,64,128,1]{2,1,0,3:T(8,128)(2,1)S(1)} %bitcast.167), kind=kOutput, calls=%fused_computation.14 | convolution fusion | flops 673710080 | bytes 22021376 | tf_op jit(solution)/shard_map/rsab,nra->rsnb/dot_general | solution.py:78
  233.7 33.0 %scatter_fusion.1 = f32[64,64,128]{2,1,0:T(8,128)S(1)} fusion(f32[64,64,128]{2,1,0:T(8,128)S(1)} %broadcast.78.clone.1, s32[320]{0:T(512)S(1)} %reshape.148, f32[320,64,128]{2,1,0:T(8,128)} %bitcast.162), kind=kCustom, calls=%fused_computation.3 | custom fusion | flops 2621440 | bytes 31458560 | tf_op jit(solution)/shard_map/scatter-add | solution.py:82
  268.0 1.6 copy.82
  269.6 16.1 %all-to-all-start.2 = ((bf16[32,64,256]{2,1,0:T(8,128)(2,1)}), bf16[32,64,256]{2,1,0:T(8,128)(2,1)S(1)}, u32[]{:S(2)}, u32[]{:S(2)}) async-start(bf16[32,64,256]{2,1,0:T(8,128)(2,1)} %copy.82), calls=%async_computation.2 | async-start | bytes 2097152 | tf_op jit(solution)/shard_map/all_to_all | solution.py:21
  285.8 5.8 cholesky.85
  293.0 4.9 custom-call.17
  297.9 2.5 all-to-all-done.2
  300.8 16.0 %psum.148 = f32[64,64]{0,1:T(8,128)S(1)} all-reduce(f32[64,64]{0,1:T(8,128)S(1)} %fusion.46), channel_id=1, replica_groups=mesh['row_0'=4,'row_1'=4,'row_2'=2,'col'=8] {'row_0'}, use_global_device_ids=true, to_apply=%region_14.19 | all-reduce | flops 4096 | bytes 32768 | tf_op jit(solution)/shard_map/psum | solution.py:26
  316.8 15.4 %psum.149 = f32[64,64]{0,1:T(8,128)S(1)} all-reduce(f32[64,64]{0,1:T(8,128)S(1)} %psum.148), channel_id=1, replica_groups=mesh['row_0'=4,'row_1'=4,'row_2'=2,'col'=8] {'row_1'}, use_global_device_ids=true, to_apply=%region_15.20 | all-reduce | flops 4096 | bytes 32768 | tf_op jit(solution)/shard_map/psum | solution.py:26
  332.3 3.4 psum.150
  335.7 27.1 %psum.151 = f32[64,64]{0,1:T(8,128)S(1)} all-reduce(f32[64,64]{0,1:T(8,128)S(1)} %psum.150), channel_id=1, replica_groups=mesh['row_0'=4,'row_1'=4,'row_2'=2,'col'=8] {'col'}, use_global_device_ids=true, to_apply=%region_17.22 | all-reduce | flops 4096 | bytes 32768 | tf_op jit(solution)/shard_map/psum | solution.py:26
  363.5 20.5 %all_to_all.25 = bf16[32,64,256]{2,1,0:T(8,128)(2,1)S(1)} all-to-all(bf16[32,64,256]{2,1,0:T(8,128)(2,1)S(1)} %broadcast_in_dim.15), channel_id=1, replica_groups=mesh['row_0'=4,'row_1'=4,'row_2'=2,'col'=8] {'row_0','row_1','row_2'}, dimensions={0} | all-to-all | bytes 2097152 | tf_op jit(solution)/shard_map/all_to_all | solution.py:37
  385.7 13.3 %gather_fusion.1 = bf16[320,64,128]{2,1,0:T(8,128)(2,1)} fusion(bf16[64,64,128]{2,0,1:T(8,128)(2,1)S(1)} %copy.87, s32[1024]{0:T(1024)S(1)} %pad_clamp_fusion), kind=kCustom, calls=%fused_computation.1.clone | custom fusion | bytes 10487040 | tf_op jit(solution)/shard_map/jit(_take)/gather | solution.py:66
  399.1 10.0 %fusion.11 = bf16[64,8,8,128]{3,2,1,0:T(8,128)(2,1)S(1)} fusion(bf16[64,5,128,128]{3,2,1,0:T(8,128)(2,1)} %param.16, bf16[64,5,64,128]{3,2,1,0:T(8,128)(2,1)} %bitcast.163, pred[64,5]{1,0:T(8,128)(4,1)S(1)} %copy.67, bf16[64,5]{1,0:T(8,128)(2,1)S(1)} %get-tuple-element.13), kind=kOutput, calls=%fused_computation.28 | convolution fusion | flops 676855808 | bytes 16778176 | tf_op jit(solution)/shard_map/rsab,nrsb->nra/dot_general | solution.py:67
  409.1 1.2 copy.123
  410.7 72.9 %all-reduce.8.cloned.1.call-done = bf16[64,8192]{1,0:T(8,128)(2,1)} async-done(((bf16[64,8192]{1,0:T(8,128)(2,1)}), bf16[64,8192]{1,0:T(8,128)(2,1)}) %all-reduce.8.cloned.1.call-update) | async-done | bytes 1048592 | tf_op jit(solution)/shard_map/psum | solution.py:110
  483.7 2.0 fusion.47
  485.6 15.5 %psum.153 = f32[64,64]{0,1:T(8,128)S(1)} all-reduce(f32[64,64]{0,1:T(8,128)S(1)} %fusion.47), channel_id=1, replica_groups=mesh['row_0'=4,'row_1'=4,'row_2'=2,'col'=8] {'row_0'}, use_global_device_ids=true, to_apply=%region_19.24 | all-reduce | flops 4096 | bytes 32768 | tf_op jit(solution)/shard_map/psum | solution.py:26
  501.1 17.0 %psum.154 = f32[64,64]{0,1:T(8,128)S(1)} all-reduce(f32[64,64]{0,1:T(8,128)S(1)} %psum.153), channel_id=1, replica_groups=mesh['row_0'=4,'row_1'=4,'row_2'=2,'col'=8] {'row_1'}, use_global_device_ids=true, to_apply=%region_20.25 | all-reduce | flops 4096 | bytes 32768 | tf_op jit(solution)/shard_map/psum | solution.py:26
  518.2 3.6 psum.155
  521.9 5.8 cholesky.96
  529.1 4.9 custom-call.19
  534.4 2.3 convolution_subtract_fusion
  536.7 1.3 copy-done.2
  538.5 10.2 %broadcast_multiply_fusion = f32[64,64,5,128]{3,1,2,0:T(8,128)} fusion(f32[64,5]{1,0:T(8,128)S(1)} %get-tuple-element.14, bf16[64,5,128,128]{3,2,1,0:T(8,128)(2,1)} %param.16, bf16[64,64,128,1]{2,1,0,3:T(8,128)(2,1)S(1)} %bitcast.165), kind=kOutput, calls=%fused_computation.13 | convolution fusion | flops 673710080 | bytes 22021376 | tf_op jit(solution)/shard_map/rsab,nra->rsnb/dot_general | solution.py:78
  548.9 33.0 %scatter_fusion.2 = f32[64,64,128]{2,1,0:T(8,128)S(1)} fusion(f32[64,64,128]{2,1,0:T(8,128)S(1)} %broadcast.78, s32[320]{0:T(512)S(1)} %reshape.148, f32[320,64,128]{2,1,0:T(8,128)} %bitcast.160), kind=kCustom, calls=%fused_computation.4 | custom fusion | flops 2621440 | bytes 31458560 | tf_op jit(solution)/shard_map/scatter-add | solution.py:82
  583.2 1.6 copy.93
  584.7 5.8 all-to-all-start.4
  590.6 5.8 cholesky.107
  597.8 4.9 custom-call.21
  602.7 1.7 constant_dynamic-slice_fusion
  604.4 0.9 convolution_add_fusion.1
  605.8 15.9 %psum.156 = f32[64,64]{1,0:T(8,128)S(1)} all-reduce(f32[64,64]{1,0:T(8,128)S(1)} %fusion.48), channel_id=1, replica_groups=mesh['row_0'=4,'row_1'=4,'row_2'=2,'col'=8] {'row_0'}, use_global_device_ids=true, to_apply=%region_24.29 | all-reduce | flops 4096 | bytes 32768 | tf_op jit(solution)/shard_map/psum | solution.py:26
  621.7 16.4 %psum.157 = f32[64,64]{1,0:T(8,128)S(1)} all-reduce(f32[64,64]{1,0:T(8,128)S(1)} %psum.156), channel_id=1, replica_groups=mesh['row_0'=4,'row_1'=4,'row_2'=2,'col'=8] {'row_1'}, use_global_device_ids=true, to_apply=%region_25.30 | all-reduce | flops 4096 | bytes 32768 | tf_op jit(solution)/shard_map/psum | solution.py:26
  638.2 3.4 psum.158
  641.6 29.1 %psum.159 = f32[64,64]{1,0:T(8,128)S(1)} all-reduce(f32[64,64]{1,0:T(8,128)S(1)} %psum.158), channel_id=1, replica_groups=mesh['row_0'=4,'row_1'=4,'row_2'=2,'col'=8] {'col'}, use_global_device_ids=true, to_apply=%region_27.32 | all-reduce | flops 4096 | bytes 32768 | tf_op jit(solution)/shard_map/psum | solution.py:26
  671.1 0.9 convolution_add_fusion
  (83 shorter events, 19.2 us)
Async XLA Ops:
  9.1 22.5 %all-to-all-start = ((bf16[32,64,256]{2,1,0:T(8,128)(2,1)}), bf16[32,64,256]{2,1,0:T(8,128)(2,1)S(1)}, u32[]{:S(2)}, u32[]{:S(2)}) async-start(bf16[32,64,256]{2,1,0:T(8,128)(2,1)} %broadcast_in_dim.13), calls=%async_computation | async-start | bytes 2097152 | tf_op jit(solution)/shard_map/all_to_all | solution.py:37
  16.7 44.7 %all-gather.2.cloned.1.call-start = ((), (), s32[]{:S(2)}) async-start(), calls=%async_computation.6 | async-start | bytes 1179648 | tf_op jit(solution)/shard_map/all_gather | solution.py:94
  18.4 119.6 %all-reduce.6.cloned.1.call-start = ((), (), s32[]{:S(2)}) async-start(), calls=%async_computation.5 | async-start | bytes 2097152 | tf_op jit(solution)/shard_map/psum | solution.py:110
  107.5 111.7 %copy-start.3 = (bf16[64,8192]{1,0:T(8,128)(2,1)S(1)}, bf16[64,8192]{1,0:T(8,128)(2,1)}, u32[]{:S(2)}) copy-start(bf16[64,8192]{1,0:T(8,128)(2,1)} %all-gather.2.cloned.1.call-done) | copy-start | bytes 3145732
  109.5 30.5 %all-to-all-start.1 = ((bf16[32,64,256]{2,1,0:T(8,128)(2,1)}), bf16[32,64,256]{2,1,0:T(8,128)(2,1)S(1)}, u32[]{:S(2)}, u32[]{:S(2)}) async-start(bf16[32,64,256]{2,1,0:T(8,128)(2,1)} %copy.77), calls=%async_computation.1 | async-start | bytes 2097152 | tf_op jit(solution)/shard_map/all_to_all | solution.py:21
  221.6 1.3 copy-start
  266.9 96.3 %copy-start.4 = (f32[64,256]{1,0:T(8,128)S(1)}, f32[64,256]{1,0:T(8,128)}, u32[]{:S(2)}) copy-start(f32[64,256]{1,0:T(8,128)} %param.15) | copy-start | bytes 196612
  269.6 30.8 %all-to-all-start.2 = ((bf16[32,64,256]{2,1,0:T(8,128)(2,1)}), bf16[32,64,256]{2,1,0:T(8,128)(2,1)S(1)}, u32[]{:S(2)}, u32[]{:S(2)}) async-start(bf16[32,64,256]{2,1,0:T(8,128)(2,1)} %copy.82), calls=%async_computation.2 | async-start | bytes 2097152 | tf_op jit(solution)/shard_map/all_to_all | solution.py:21
  285.7 198.0 %all-reduce.8.cloned.1.call-start = ((), (), s32[]{:S(2)}) async-start(), calls=%async_computation.7 | async-start | bytes 2097152 | tf_op jit(solution)/shard_map/psum | solution.py:110
  399.1 11.3 %copy-start.5 = (f32[64,256]{1,0:T(8,128)S(1)}, f32[64,256]{1,0:T(8,128)}, u32[]{:S(2)}) copy-start(f32[64,256]{1,0:T(8,128)} %param.13) | copy-start | bytes 196612
  409.1 125.3 %copy-start.1 = (f32[64,8192]{1,0:T(8,128)S(1)}, f32[64,8192]{1,0:T(8,128)}, u32[]{:S(2)}) copy-start(f32[64,8192]{1,0:T(8,128)} %copy-done) | copy-start | bytes 6291460
  536.7 1.3 copy-start.2
  584.7 20.7 %all-to-all-start.4 = ((bf16[32,64,256]{2,1,0:T(8,128)(2,1)}), bf16[32,64,256]{2,1,0:T(8,128)(2,1)S(1)}, u32[]{:S(2)}, u32[]{:S(2)}) async-start(bf16[32,64,256]{2,1,0:T(8,128)(2,1)} %copy.93), calls=%async_computation.4 | async-start | bytes 2097152 | tf_op jit(solution)/shard_map/all_to_all | solution.py:21
Sparse Core Ops, SparseCore 0:
  19.9 41.4 all-gather.1
  63.8 74.1 all-reduce.5
  410.5 73.1 all-reduce.7
where the time goes:
time: 692 us; the launch traced here: 679 us
  blocking collectives  250 us (36%)
  other arithmetic  154 us (22%)
  waiting for transfers between devices  110 us (16%)
  matrix products  63.6 us (9%)
  local copies, waits for them, and re-layouts  50.2 us (7%)
  starting transfers between devices  37 us (5%)
  between operations  14.8 us (2%)
    psum x15, blocking collectives, over_axes(): return functools.reduce(lax.psum, axes, value)  229 us
    scatter-add x3, other arithmetic, gradients(): jax.ops.segment_sum(contrib.reshape(-1, rhs_count, tile_width), tile_bloc...  99.3 us
    psum x2, waiting for transfers between devices, per_device(): lax.psum(image_partial_term.astype(jnp.bfloat16), 'col').astype(jnp.float32)  94 us
    dot_general x3, matrix products, gradients(): jnp.einsum('rsab,nra->rsnb', jacobian_tiles, row_view, preferred_element_...  30.5 us
    all_to_all x3, starting transfers between devices, sent_and_summed(): lax.all_to_all(in_blocks(value, dim, devices), axis, 0, 0, tiled=True)  29.3 us
    gather x2, local copies, waits for them, and re-layouts, images(): jnp.take(table_view, tile_blocks, axis=1) * live_slot[None, :, :, None]  26.7 us
    another operation x12, other arithmetic, solve_spd(): factor_low = jnp.linalg.cholesky(matrix)  26.1 us
    another operation x8, other arithmetic, solve_spd(): lax.linalg.triangular_solve(factor_low, middle, left_side=True, lower=Tru...  22.2 us
  transfers between devices with their start and end apart: 7, of which 6 were waited for; matrix products, arithmetic and copies ran while one was open for 16% of the time, Pallas kernels for 0%

commit v1 on v0

--- a/solution.py
+++ b/solution.py
@@ -107,7 +107,9 @@
     for iteration in range(ITERS):
         direction_half = collect(direction.astype(jnp.bfloat16), ROW, 1)
         image_partial_term = images(jacobian_tiles, tile_blocks, live_slot, direction_half)
-        image = lax.psum(image_partial_term.astype(jnp.bfloat16), "col").astype(jnp.float32)
+        image = jnp.sum(
+            lax.all_gather(image_partial_term.astype(jnp.bfloat16), "col"), axis=0
+        ).astype(jnp.float32)
         curvature = over_axes(gram_matrix(image), ROW)
         image, curvature = (image, curvature)
         step_alpha = solve_spd(curvature, gamma_now)

time: 692 us -> 723 us (1.045)
  waiting for transfers between devices: 110 us -> 133 us
  blocking collectives: 250 us -> 270 us
  starting transfers between devices: 37 us -> 19.4 us
  other arithmetic: 154 us -> 163 us
    all_gather x0 -> x2, waiting for transfers between devices: none -> 117 us  [per_device(): lax.all_gather(image_partial_term.astype(jnp.bfloat16), 'col')]
    psum x2 -> x0, waiting for transfers between devices: 94 us -> none  [per_device(): lax.psum(image_partial_term.astype(jnp.bfloat16), 'col').astype(jnp.float32)]
    all_to_all x0 -> x1, blocking collectives: none -> 22.1 us  [sent_and_summed(): lax.all_to_all(in_blocks(value, dim, devices), axis, 0, 0, tiled=True)]
    all_to_all x3 -> x2, starting transfers between devices: 29.3 us -> 11.7 us  [sent_and_summed(): lax.all_to_all(in_blocks(value, dim, devices), axis, 0, 0, tiled=True)]
    reduce_sum x0 -> x2, other arithmetic: none -> 9.9 us  [per_device(): jnp.sum(lax.all_gather(image_partial_term.astype(jnp.bfloat16), 'col'), a...]
  transfers between devices with their start and end apart: 7 -> 6, of which waited for: 6 -> 6; matrix products, arithmetic and copies ran while one was open for 16% -> 15% of each run, Pallas kernels for 0% -> 0%
where the time goes in v1:
time: 723 us; the launch traced here: 709 us
  blocking collectives  270 us (37%)
  other arithmetic  163 us (23%)
  waiting for transfers between devices  133 us (18%)
  matrix products  58.1 us (8%)
  local copies, waits for them, and re-layouts  50.1 us (7%)
  starting transfers between devices  19.4 us (3%)
  between operations  14.8 us (2%)
    psum x15, blocking collectives, over_axes(): return functools.reduce(lax.psum, axes, value)  228 us
    all_gather x2, waiting for transfers between devices, per_device(): lax.all_gather(image_partial_term.astype(jnp.bfloat16), 'col')  117 us
    scatter-add x3, other arithmetic, gradients(): jax.ops.segment_sum(contrib.reshape(-1, rhs_count, tile_width), tile_bloc...  99.1 us
    dot_general x3, matrix products, gradients(): jnp.einsum('rsab,nra->rsnb', jacobian_tiles, row_view, preferred_element_...  30.5 us
    gather x2, local copies, waits for them, and re-layouts, images(): jnp.take(table_view, tile_blocks, axis=1) * live_slot[None, :, :, None]  26.7 us
    another operation x12, other arithmetic, solve_spd(): factor_low = jnp.linalg.cholesky(matrix)  26.1 us
    another operation x8, other arithmetic, solve_spd(): lax.linalg.triangular_solve(factor_low, middle, left_side=True, lower=Tru...  22.2 us
    all_to_all x1, blocking collectives, sent_and_summed(): lax.all_to_all(in_blocks(value, dim, devices), axis, 0, 0, tiled=True)  22.1 us
  transfers between devices with their start and end apart: 6, of which 6 were waited for; matrix products, arithmetic and copies ran while one was open for 15% of the time, Pallas kernels for 0%

profile of v1, /device:TPU:4, one launch (start us, length us, event | category | flops | bytes accessed | tf_op | source)
XLA Modules:
  0.0 709.3 jit_solution(13776926576667168792)
XLA Ops:
  7.2 0.8 convert_element_type.116
  8.0 1.1 broadcast_in_dim.13
  9.1 7.6 %all-to-all-start = ((bf16[32,64,256]{2,1,0:T(8,128)(2,1)}), bf16[32,64,256]{2,1,0:T(8,128)(2,1)S(1)}, u32[]{:S(2)}, u32[]{:S(2)}) async-start(bf16[32,64,256]{2,1,0:T(8,128)(2,1)} %broadcast_in_dim.13), calls=%async_computation | async-start | bytes 2097152 | tf_op jit(solution)/shard_map/all_to_all | solution.py:37
  16.8 1.6 convert_element_type.121
  18.5 0.7 compare_select_fusion
  19.4 0.7 compare_and_fusion
  20.2 0.7 fusion.39
  21.0 10.6 %all-to-all-done = bf16[32,64,256]{2,1,0:T(8,128)(2,1)S(1)} async-done(((bf16[32,64,256]{2,1,0:T(8,128)(2,1)}), bf16[32,64,256]{2,1,0:T(8,128)(2,1)S(1)}, u32[]{:S(2)}, u32[]{:S(2)}) %all-to-all-start) | async-done | bytes 1048608 | tf_op jit(solution)/shard_map/all_to_all | solution.py:37
  33.3 13.3 %gather_fusion = bf16[320,64,128]{2,1,0:T(8,128)(2,1)} fusion(bf16[64,64,128]{2,0,1:T(8,128)(2,1)S(1)} %copy.70, s32[1024]{0:T(1024)S(1)} %pad_clamp_fusion), kind=kCustom, calls=%fused_computation.clone | custom fusion | bytes 10487040 | tf_op jit(solution)/shard_map/jit(_take)/gather | solution.py:66
  46.6 10.1 %fusion.10 = bf16[64,64,128]{2,0,1:T(8,128)(2,1)S(1)} fusion(bf16[64,5,128,128]{3,2,1,0:T(8,128)(2,1)} %param.16, bf16[64,5,64,128]{3,2,1,0:T(8,128)(2,1)} %bitcast.156, pred[64,5]{1,0:T(8,128)(4,1)S(1)} %copy.67, bf16[64,5]{1,0:T(8,128)(2,1)S(1)} %get-tuple-element.13), kind=kOutput, calls=%fused_computation.27 | convolution fusion | flops 676855808 | bytes 16778176 | tf_op jit(solution)/shard_map/rsab,nrsb->nra/dot_general | solution.py:67
  56.7 0.7 copy.71
  57.4 1.3 convert_element_type.120
  58.9 2.5 all-gather.6.cloned.1.call-done
  61.4 1.5 copy.110
  62.9 10.2 %broadcast_multiply_fusion.2 = f32[64,64,5,128]{3,1,2,0:T(8,128)} fusion(f32[64,5]{1,0:T(8,128)S(1)} %get-tuple-element.14, bf16[64,5,128,128]{3,2,1,0:T(8,128)(2,1)} %param.16, bf16[64,64,128,1]{2,1,0,3:T(8,128)(2,1)S(1)} %bitcast.158), kind=kOutput, calls=%fused_computation.15 | convolution fusion | flops 673710080 | bytes 22021376 | tf_op jit(solution)/shard_map/rsab,nra->rsnb/dot_general | solution.py:78
  73.3 33.1 %scatter_fusion = f32[64,64,128]{2,1,0:T(8,128)S(1)} fusion(f32[64,64,128]{2,1,0:T(8,128)S(1)} %broadcast.78.clone, s32[320]{0:T(512)S(1)} %reshape.168, f32[320,64,128]{2,1,0:T(8,128)} %bitcast.153), kind=kCustom, calls=%fused_computation.2 | custom fusion | flops 2621440 | bytes 31458560 | tf_op jit(solution)/shard_map/scatter-add | solution.py:82
  108.3 22.1 %all_to_all.25 = bf16[32,64,256]{2,1,0:T(8,128)(2,1)S(1)} all-to-all(bf16[32,64,256]{2,1,0:T(8,128)(2,1)S(1)} %copy.77), channel_id=1, replica_groups=mesh['row_0'=4,'row_1'=4,'row_2'=2,'col'=8] {'row_0','row_1','row_2'}, dimensions={0} | all-to-all | bytes 2097152 | tf_op jit(solution)/shard_map/all_to_all | solution.py:21
  130.7 25.0 %all-gather.4.cloned.1.call-done = bf16[8,64,8192]{2,1,0:T(8,128)(2,1)} async-done(((bf16[1,64,8192]{2,1,0:T(8,128)(2,1)}), bf16[8,64,8192]{2,1,0:T(8,128)(2,1)}) %all-gather.4.cloned.1.call-update) | async-done | bytes 8388624 | tf_op jit(solution)/shard_map/all_gather | solution.py:111
  155.7 5.0 reduce_sum.51
  161.1 16.0 %all-reduce.1 = (f32[64,64]{0,1:T(8,128)S(1)}, f32[64,64]{0,1:T(8,128)S(1)}) all-reduce(f32[64,64]{0,1:T(8,128)S(1)} %fusion.45, f32[64,64]{0,1:T(8,128)S(1)} %fusion.44), channel_id=1, replica_groups=mesh['row_0'=4,'row_1'=4,'row_2'=2,'col'=8] {'row_0'}, use_global_device_ids=true, to_apply=%region_8.0 | all-reduce | flops 8192 | bytes 65536 | tf_op jit(solution)/shard_map/psum | solution.py:26
  177.0 17.7 %all-reduce = (f32[64,64]{0,1:T(8,128)S(1)}, f32[64,64]{0,1:T(8,128)S(1)}) all-reduce(f32[64,64]{0,1:T(8,128)S(1)} %get-tuple-element.9, f32[64,64]{0,1:T(8,128)S(1)} %get-tuple-element.10), channel_id=1, replica_groups=mesh['row_0'=4,'row_1'=4,'row_2'=2,'col'=8] {'row_1'}, use_global_device_ids=true, to_apply=%region_9.0 | all-reduce | flops 8192 | bytes 65536 | tf_op jit(solution)/shard_map/psum | solution.py:26
  194.7 3.6 all-reduce.2
  198.3 28.3 %psum.132 = f32[64,64]{0,1:T(8,128)S(1)} all-reduce(f32[64,64]{0,1:T(8,128)S(1)} %get-tuple-element.11), channel_id=1, replica_groups=mesh['row_0'=4,'row_1'=4,'row_2'=2,'col'=8] {'col'}, use_global_device_ids=true, to_apply=%region_11.14 | all-reduce | flops 4096 | bytes 32768 | tf_op jit(solution)/shard_map/psum | solution.py:26
  226.7 5.8 cholesky.74
  233.9 4.9 custom-call.15
  239.2 1.1 convolution_subtract_fusion.1
  240.3 1.3 copy-done
  242.1 10.2 %broadcast_multiply_fusion.1 = f32[64,64,5,128]{3,1,2,0:T(8,128)} fusion(f32[64,5]{1,0:T(8,128)S(1)} %get-tuple-element.14, bf16[64,5,128,128]{3,2,1,0:T(8,128)(2,1)} %param.16, bf16[64,64,128,1]{2,1,0,3:T(8,128)(2,1)S(1)} %bitcast.159), kind=kOutput, calls=%fused_computation.14 | convolution fusion | flops 673710080 | bytes 22021376 | tf_op jit(solution)/shard_map/rsab,nra->rsnb/dot_general | solution.py:78
  252.5 33.0 %scatter_fusion.1 = f32[64,64,128]{2,1,0:T(8,128)S(1)} fusion(f32[64,64,128]{2,1,0:T(8,128)S(1)} %broadcast.78.clone.1, s32[320]{0:T(512)S(1)} %reshape.168, f32[320,64,128]{2,1,0:T(8,128)} %bitcast.154), kind=kCustom, calls=%fused_computation.3 | custom fusion | flops 2621440 | bytes 31458560 | tf_op jit(solution)/shard_map/scatter-add | solution.py:82
  286.8 1.6 copy.82
  288.4 5.9 all-to-all-start.2
  294.4 5.8 cholesky.85
  301.6 4.9 custom-call.17
  306.4 2.6 all-to-all-done.2
  309.4 15.9 %psum.133 = f32[64,64]{0,1:T(8,128)S(1)} all-reduce(f32[64,64]{0,1:T(8,128)S(1)} %fusion.46), channel_id=1, replica_groups=mesh['row_0'=4,'row_1'=4,'row_2'=2,'col'=8] {'row_0'}, use_global_device_ids=true, to_apply=%region_14.19 | all-reduce | flops 4096 | bytes 32768 | tf_op jit(solution)/shard_map/psum | solution.py:26
  325.4 15.5 %psum.134 = f32[64,64]{0,1:T(8,128)S(1)} all-reduce(f32[64,64]{0,1:T(8,128)S(1)} %psum.133), channel_id=1, replica_groups=mesh['row_0'=4,'row_1'=4,'row_2'=2,'col'=8] {'row_1'}, use_global_device_ids=true, to_apply=%region_15.20 | all-reduce | flops 4096 | bytes 32768 | tf_op jit(solution)/shard_map/psum | solution.py:26
  340.8 3.4 psum.135
  344.3 27.1 %psum.136 = f32[64,64]{0,1:T(8,128)S(1)} all-reduce(f32[64,64]{0,1:T(8,128)S(1)} %psum.135), channel_id=1, replica_groups=mesh['row_0'=4,'row_1'=4,'row_2'=2,'col'=8] {'col'}, use_global_device_ids=true, to_apply=%region_17.22 | all-reduce | flops 4096 | bytes 32768 | tf_op jit(solution)/shard_map/psum | solution.py:26
  372.1 20.7 %all_to_all.26 = bf16[32,64,256]{2,1,0:T(8,128)(2,1)S(1)} all-to-all(bf16[32,64,256]{2,1,0:T(8,128)(2,1)S(1)} %broadcast_in_dim.15), channel_id=1, replica_groups=mesh['row_0'=4,'row_1'=4,'row_2'=2,'col'=8] {'row_0','row_1','row_2'}, dimensions={0} | all-to-all | bytes 2097152 | tf_op jit(solution)/shard_map/all_to_all | solution.py:37
  394.5 13.3 %gather_fusion.1 = bf16[320,64,128]{2,1,0:T(8,128)(2,1)} fusion(bf16[64,64,128]{2,0,1:T(8,128)(2,1)S(1)} %copy.87, s32[1024]{0:T(1024)S(1)} %pad_clamp_fusion), kind=kCustom, calls=%fused_computation.1.clone | custom fusion | bytes 10487040 | tf_op jit(solution)/shard_map/jit(_take)/gather | solution.py:66
  407.8 10.0 %fusion.11 = bf16[64,64,128]{2,0,1:T(8,128)(2,1)S(1)} fusion(bf16[64,5,128,128]{3,2,1,0:T(8,128)(2,1)} %param.16, bf16[64,5,64,128]{3,2,1,0:T(8,128)(2,1)} %bitcast.155, pred[64,5]{1,0:T(8,128)(4,1)S(1)} %copy.67, bf16[64,5]{1,0:T(8,128)(2,1)S(1)} %get-tuple-element.13), kind=kOutput, calls=%fused_computation.28 | convolution fusion | flops 676855808 | bytes 16778176 | tf_op jit(solution)/shard_map/rsab,nrsb->nra/dot_general | solution.py:67
  418.6 1.4 convert_element_type.136
  420.3 92.3 %all-gather.8.cloned.1.call-done = bf16[8,64,8192]{2,1,0:T(8,128)(2,1)} async-done(((bf16[1,64,8192]{2,1,0:T(8,128)(2,1)}), bf16[8,64,8192]{2,1,0:T(8,128)(2,1)}) %all-gather.8.cloned.1.call-update) | async-done | bytes 8388624 | tf_op jit(solution)/shard_map/all_gather | solution.py:111
  512.6 5.0 reduce_sum.54
  518.0 15.8 %psum.137 = f32[64,64]{0,1:T(8,128)S(1)} all-reduce(f32[64,64]{0,1:T(8,128)S(1)} %fusion.47), channel_id=1, replica_groups=mesh['row_0'=4,'row_1'=4,'row_2'=2,'col'=8] {'row_0'}, use_global_device_ids=true, to_apply=%region_19.24 | all-reduce | flops 4096 | bytes 32768 | tf_op jit(solution)/shard_map/psum | solution.py:26
  533.8 17.0 %psum.138 = f32[64,64]{0,1:T(8,128)S(1)} all-reduce(f32[64,64]{0,1:T(8,128)S(1)} %psum.137), channel_id=1, replica_groups=mesh['row_0'=4,'row_1'=4,'row_2'=2,'col'=8] {'row_1'}, use_global_device_ids=true, to_apply=%region_20.25 | all-reduce | flops 4096 | bytes 32768 | tf_op jit(solution)/shard_map/psum | solution.py:26
  550.8 3.4 psum.139
  554.3 5.8 cholesky.96
  561.5 4.9 custom-call.19
  566.9 1.1 convolution_subtract_fusion
  567.9 1.3 copy-done.2
  569.7 10.2 %broadcast_multiply_fusion = f32[64,64,5,128]{3,1,2,0:T(8,128)} fusion(f32[64,5]{1,0:T(8,128)S(1)} %get-tuple-element.14, bf16[64,5,128,128]{3,2,1,0:T(8,128)(2,1)} %param.16, bf16[64,64,128,1]{2,1,0,3:T(8,128)(2,1)S(1)} %bitcast.157), kind=kOutput, calls=%fused_computation.13 | convolution fusion | flops 673710080 | bytes 22021376 | tf_op jit(solution)/shard_map/rsab,nra->rsnb/dot_general | solution.py:78
  580.1 33.0 %scatter_fusion.2 = f32[64,64,128]{2,1,0:T(8,128)S(1)} fusion(f32[64,64,128]{2,1,0:T(8,128)S(1)} %broadcast.78, s32[320]{0:T(512)S(1)} %reshape.168, f32[320,64,128]{2,1,0:T(8,128)} %bitcast.152), kind=kCustom, calls=%fused_computation.4 | custom fusion | flops 2621440 | bytes 31458560 | tf_op jit(solution)/shard_map/scatter-add | solution.py:82
  614.4 1.6 copy.93
  615.9 5.8 all-to-all-start.4
  621.8 5.8 cholesky.107
  629.0 4.9 custom-call.21
  633.9 1.7 constant_dynamic-slice_fusion
  635.6 0.9 convolution_add_fusion.1
  637.0 15.9 %psum.140 = f32[64,64]{1,0:T(8,128)S(1)} all-reduce(f32[64,64]{1,0:T(8,128)S(1)} %fusion.48), channel_id=1, replica_groups=mesh['row_0'=4,'row_1'=4,'row_2'=2,'col'=8] {'row_0'}, use_global_device_ids=true, to_apply=%region_24.29 | all-reduce | flops 4096 | bytes 32768 | tf_op jit(solution)/shard_map/psum | solution.py:26
  652.9 16.4 %psum.141 = f32[64,64]{1,0:T(8,128)S(1)} all-reduce(f32[64,64]{1,0:T(8,128)S(1)} %psum.140), channel_id=1, replica_groups=mesh['row_0'=4,'row_1'=4,'row_2'=2,'col'=8] {'row_1'}, use_global_device_ids=true, to_apply=%region_25.30 | all-reduce | flops 4096 | bytes 32768 | tf_op jit(solution)/shard_map/psum | solution.py:26
  669.4 3.4 psum.142
  672.8 28.3 %psum.143 = f32[64,64]{1,0:T(8,128)S(1)} all-reduce(f32[64,64]{1,0:T(8,128)S(1)} %psum.142), channel_id=1, replica_groups=mesh['row_0'=4,'row_1'=4,'row_2'=2,'col'=8] {'col'}, use_global_device_ids=true, to_apply=%region_27.32 | all-reduce | flops 4096 | bytes 32768 | tf_op jit(solution)/shard_map/psum | solution.py:26
  701.5 0.9 convolution_add_fusion
  (88 shorter events, 20.7 us)
Async XLA Ops:
  9.1 22.5 %all-to-all-start = ((bf16[32,64,256]{2,1,0:T(8,128)(2,1)}), bf16[32,64,256]{2,1,0:T(8,128)(2,1)S(1)}, u32[]{:S(2)}, u32[]{:S(2)}) async-start(bf16[32,64,256]{2,1,0:T(8,128)(2,1)} %broadcast_in_dim.13), calls=%async_computation | async-start | bytes 2097152 | tf_op jit(solution)/shard_map/all_to_all | solution.py:37
  16.7 44.7 %all-gather.6.cloned.1.call-start = ((), (), s32[]{:S(2)}) async-start(), calls=%async_computation.6 | async-start | bytes 1179648 | tf_op jit(solution)/shard_map/all_gather | solution.py:94
  18.4 137.3 %all-gather.4.cloned.1.call-start = ((), (), s32[]{:S(2)}) async-start(), calls=%async_computation.5 | async-start | bytes 9437184 | tf_op jit(solution)/shard_map/all_gather | solution.py:111
  56.7 2.0 copy-start.6
  130.7 108.5 %copy-start.3 = (bf16[64,8192]{1,0:T(8,128)(2,1)S(1)}, bf16[64,8192]{1,0:T(8,128)(2,1)}, u32[]{:S(2)}) copy-start(bf16[64,8192]{1,0:T(8,128)(2,1)} %all-gather.6.cloned.1.call-done) | copy-start | bytes 3145732
  240.3 1.3 copy-start
  285.7 86.1 %copy-start.4 = (f32[64,256]{1,0:T(8,128)S(1)}, f32[64,256]{1,0:T(8,128)}, u32[]{:S(2)}) copy-start(f32[64,256]{1,0:T(8,128)} %param.15) | copy-start | bytes 196612
  288.4 20.7 %all-to-all-start.2 = ((bf16[32,64,256]{2,1,0:T(8,128)(2,1)}), bf16[32,64,256]{2,1,0:T(8,128)(2,1)S(1)}, u32[]{:S(2)}, u32[]{:S(2)}) async-start(bf16[32,64,256]{2,1,0:T(8,128)(2,1)} %copy.82), calls=%async_computation.2 | async-start | bytes 2097152 | tf_op jit(solution)/shard_map/all_to_all | solution.py:21
  294.2 218.4 %all-gather.8.cloned.1.call-start = ((), (), s32[]{:S(2)}) async-start(), calls=%async_computation.7 | async-start | bytes 9437184 | tf_op jit(solution)/shard_map/all_gather | solution.py:111
  417.9 2.1 copy-start.5
  420.3 146.6 %copy-start.1 = (f32[64,8192]{1,0:T(8,128)S(1)}, f32[64,8192]{1,0:T(8,128)}, u32[]{:S(2)}) copy-start(f32[64,8192]{1,0:T(8,128)} %copy-done) | copy-start | bytes 6291460
  567.9 1.3 copy-start.2
  615.9 20.7 %all-to-all-start.4 = ((bf16[32,64,256]{2,1,0:T(8,128)(2,1)}), bf16[32,64,256]{2,1,0:T(8,128)(2,1)S(1)}, u32[]{:S(2)}, u32[]{:S(2)}) async-start(bf16[32,64,256]{2,1,0:T(8,128)(2,1)} %copy.93), calls=%async_computation.4 | async-start | bytes 2097152 | tf_op jit(solution)/shard_map/all_to_all | solution.py:21
Sparse Core Ops, SparseCore 0:
  19.9 41.4 all-gather.5
  63.2 92.4 all-gather.3
  420.0 92.5 all-gather.7
